TPU v7x, 256 devices: a whole 4x4x8 slice. The times are simulated.
256 devices in a mesh: ctx: 32 (over z_lo, y, x), exp: 8 (over z_hi, core).
Axes of the slice: x: 4, y: 4, z: 8 (z_hi: 4, z_lo: 2; z = z_hi * 2 + z_lo), core: 2. Of those that a mesh axis runs over, the one named last changes fastest.
Arguments:
- tokens: bfloat16 [4096, 2880], P('ctx'), may hold values from -6 to 6
- cotangent: bfloat16 [4096, 2880], P('ctx'), may hold values from -6 to 6
- expert_ids: int32 [4096, 4], P('ctx'), may hold values from 0 to 31, all different within a row; in each aligned block of 128 rows (0 to 127, 128 to 255, ...) at most 20 rows name the same one
- combine_weights: float32 [4096, 4], P('ctx'), may hold values from 0.05 to 1
- w_query: bfloat16 [2880, 2048], P('ctx', 'exp'), may hold values from -0.109375 to 0.109375
- key_value_weight: bfloat16 [2880, 1024], P('ctx', 'exp'), may hold values from -0.109375 to 0.109375
- w_output: bfloat16 [2048, 2880], P('exp', 'ctx'), may hold values from -0.125 to 0.125
- w_gate: bfloat16 [32, 2880, 2048], P('ctx', None, 'exp'), may hold values from -0.109375 to 0.109375
- w_up: bfloat16 [32, 2880, 2048], P('ctx', None, 'exp'), may hold values from -0.109375 to 0.109375
- w_down: bfloat16 [32, 2048, 2880], P('ctx', 'exp'), may hold values from -0.125 to 0.125
Outputs:
- block_out: bfloat16 [4096, 2880], P('ctx')
- grad_tokens: bfloat16 [4096, 2880], P('ctx')
- grad_query: bfloat16 [2880, 2048], P('ctx', 'exp')
- grad_keyval: bfloat16 [2880, 1024], P('ctx', 'exp')
- grad_output: bfloat16 [2048, 2880], P('exp', 'ctx')
- grad_gate: bfloat16 [32, 2880, 2048], P('ctx', None, 'exp')
- grad_up: bfloat16 [32, 2880, 2048], P('ctx', None, 'exp')
- grad_down: bfloat16 [32, 2048, 2880], P('ctx', 'exp')
Inputs may be any that keep to these rules, and one draw needn't show every extreme that they name: `expert_ids`: each row names 4 different experts. Within the 128 rows of one context block no expert is named more than 20 times, and in some block one expert is named exactly 20 times.
All inputs are finite; a program needn't handle non-finite values.
Results may differ from a plain program's by a relative error of at most 0.029.
Values may be sent and summed in bfloat16 or wider, within the bound.
A program may use at most 128 MiB of HBM per device.

v0:
```python
import jax
import jax.numpy as jnp
from jax import lax
from jax.sharding import PartitionSpec as P

QUERY_HEADS = 32
KEY_VALUE_HEADS = 8
HEAD_SIZE = 64
WINDOW = 128
EPSILON = 1e-05
GLU_ALPHA = 1.702


def shifted(shard, axis, by):
    size = lax.axis_size(axis)
    pairs = [(i, i + by) for i in range(size) if 0 <= i + by < size]
    return lax.ppermute(shard, axis, pairs)


def rms_norm(values):
    inv_rms = lax.rsqrt(jnp.mean(values * values, axis=-1, keepdims=True) + EPSILON)
    return (values * inv_rms, inv_rms)


def rms_back(values, inv_rms, grad_in):
    inner_mean = jnp.mean(grad_in * values, axis=-1, keepdims=True)
    return inv_rms * grad_in - values * (inv_rms * inv_rms * inv_rms) * inner_mean


def rounded(values):
    return lax.optimization_barrier(values.astype(jnp.bfloat16)).astype(jnp.float32)


def band_valid(row_count, band_width, block_idx):
    query_pos = block_idx * row_count + jnp.arange(row_count)[:, None]
    key_pos = block_idx * row_count - band_width + jnp.arange(band_width + row_count)[None, :]
    return (key_pos <= query_pos) & (key_pos > query_pos - band_width) & (key_pos >= 0)


def attend(query_matrix, key_value, valid_mask):
    key_rows = key_value[:, :, 0]
    value_rows = key_value[:, :, 1]
    scores = (
        jnp.einsum("tgjd,sgd->gjts", query_matrix, key_rows, preferred_element_type=jnp.float32)
        * 0.125
    )
    weights = jnp.where(valid_mask, jnp.exp(scores), 0.0)
    probability_single = weights / jnp.sum(weights, axis=-1, keepdims=True)
    probability_half = probability_single.astype(jnp.bfloat16)
    attended = jnp.einsum(
        "gjts,sgd->tgjd", probability_half, value_rows, preferred_element_type=jnp.float32
    )
    return (attended.astype(jnp.bfloat16), probability_single, probability_half)


def attention_backward(query_matrix, key_value, probability_single, probability_half, grad_out):
    key_rows = key_value[:, :, 0]
    value_rows = key_value[:, :, 1]
    grad_prob = jnp.einsum(
        "tgjd,sgd->gjts", grad_out, value_rows, preferred_element_type=jnp.float32
    )
    grad_value = jnp.einsum(
        "gjts,tgjd->sgd", probability_half, grad_out, preferred_element_type=jnp.float32
    )
    grad_score = (
        probability_single
        * (grad_prob - jnp.sum(grad_prob * probability_single, axis=-1, keepdims=True))
        * 0.125
    ).astype(jnp.bfloat16)
    query_gradients = jnp.einsum(
        "gjts,sgd->tgjd", grad_score, key_rows, preferred_element_type=jnp.float32
    )
    grad_key = jnp.einsum(
        "gjts,tgjd->sgd", grad_score, query_matrix, preferred_element_type=jnp.float32
    )
    return (query_gradients, jnp.stack([grad_key, grad_value], axis=2))


def place_routes(flat_ids, expert_count, capacity):
    one_hot = (flat_ids[:, None] == jnp.arange(expert_count)[None, :]).astype(jnp.int32)
    earlier = jnp.cumsum(one_hot, axis=0) - one_hot
    return flat_ids * capacity + jnp.sum(earlier * one_hot, axis=1)


def pick_rows(returned, route_table):
    feature_count = returned.shape[-1]
    flat_slots = returned.reshape(-1, feature_count)
    return jnp.einsum("tks,sd->tkd", route_table, flat_slots, preferred_element_type=jnp.float32)


def sum_heads(values):
    return lax.psum(values.astype(jnp.bfloat16), "exp").astype(jnp.float32)


def over_experts(buffer):
    return lax.all_to_all(buffer, "ctx", split_axis=0, concat_axis=0, tiled=True)


def back_from_experts(buffer):
    return lax.all_to_all(buffer, "ctx", split_axis=0, concat_axis=0, tiled=True)


def body(
    tokens,
    cotangent,
    expert_ids,
    combine_weights,
    w_query,
    key_value_weight,
    w_output,
    w_gate,
    w_up,
    w_down,
):
    row_count, model_width = tokens.shape
    top_count = expert_ids.shape[1]
    ctx_count = lax.axis_size("ctx")
    ctx_block = lax.axis_index("ctx")
    capacity = row_count * top_count * 5 // (4 * ctx_count)
    kv_heads = key_value_weight.shape[1] // (2 * HEAD_SIZE)
    query_head_group = QUERY_HEADS // KEY_VALUE_HEADS
    tokens_f32 = tokens.astype(jnp.float32)
    normed_f32, token_scale = rms_norm(tokens_f32)
    normed = normed_f32.astype(jnp.bfloat16)
    full_query, full_keyval, full_output = (
        lax.all_gather(w_query, "ctx", axis=0, tiled=True),
        lax.all_gather(key_value_weight, "ctx", axis=0, tiled=True),
        lax.all_gather(w_output, "ctx", axis=1, tiled=True),
    )
    query_matrix = jnp.dot(normed, full_query, preferred_element_type=jnp.float32).astype(
        jnp.bfloat16
    )
    key_value = jnp.dot(normed, full_keyval, preferred_element_type=jnp.float32).astype(
        jnp.bfloat16
    )
    prev_rim = shifted(key_value, "ctx", 1)
    query_heads = query_matrix.reshape(row_count, kv_heads, query_head_group, HEAD_SIZE)
    banded_key_span = jnp.concatenate([prev_rim, key_value], axis=0).reshape(
        WINDOW + row_count, kv_heads, 2, HEAD_SIZE
    )
    valid_mask = band_valid(row_count, WINDOW, ctx_block)
    attended, probability_single, probability_half = attend(
        query_heads, banded_key_span, valid_mask
    )
    attended_flat = attended.reshape(row_count, -1)
    head_part = jnp.dot(attended_flat, full_output, preferred_element_type=jnp.float32)
    residual = (tokens_f32 + sum_heads(head_part)).astype(jnp.bfloat16)
    moe_f32, resid_scale = rms_norm(residual.astype(jnp.float32))
    moe_input = moe_f32.astype(jnp.bfloat16)
    residual_f32 = residual.astype(jnp.float32)
    slot_count = ctx_count * capacity
    target = place_routes(expert_ids.reshape(-1), ctx_count, capacity)
    route_table = (
        (target[:, None] == jnp.arange(slot_count)[None, :])
        .astype(jnp.bfloat16)
        .reshape(row_count, top_count, slot_count)
    )
    slot_token = jnp.sum(route_table, axis=1)
    outgoing = jnp.dot(slot_token.T, moe_input, preferred_element_type=jnp.float32).astype(
        jnp.bfloat16
    )
    incoming = over_experts(outgoing.reshape(ctx_count, capacity, model_width))
    expert_rows = incoming.reshape(-1, model_width)
    gate_pre = jnp.dot(expert_rows, w_gate[0], preferred_element_type=jnp.float32)
    up_pre = jnp.dot(expert_rows, w_up[0], preferred_element_type=jnp.float32)
    gate_sig = jax.nn.sigmoid(GLU_ALPHA * gate_pre)
    gate_glu = gate_pre * gate_sig
    activated = (gate_glu * (up_pre + 1.0)).astype(jnp.bfloat16)
    down_part = (
        jnp.dot(activated, w_down[0], preferred_element_type=jnp.float32)
        .astype(jnp.bfloat16)
        .reshape(ctx_count, capacity, model_width)
    )
    route_scale = combine_weights[:, :, None]
    returned = back_from_experts(down_part)
    moe_total = sum_heads(jnp.sum(pick_rows(returned, route_table) * route_scale, axis=1))
    block_out = (residual_f32 + moe_total).astype(jnp.bfloat16)
    cot_f32 = cotangent.astype(jnp.float32)
    grad_rows = (route_scale * cot_f32[:, None, :]).astype(jnp.bfloat16)
    grad_sent = jnp.einsum(
        "tks,tkd->sd", route_table, grad_rows, preferred_element_type=jnp.float32
    ).astype(jnp.bfloat16)
    grad_expert = over_experts(grad_sent.reshape(ctx_count, capacity, model_width)).reshape(
        -1, model_width
    )
    grad_act = jnp.dot(grad_expert, w_down[0].T, preferred_element_type=jnp.float32)
    grad_gate_pre = (
        grad_act * (up_pre + 1.0) * (gate_sig + GLU_ALPHA * gate_glu * (1.0 - gate_sig))
    ).astype(jnp.bfloat16)
    grad_up_pre = (grad_act * gate_glu).astype(jnp.bfloat16)
    grad_down = jnp.dot(activated.T, grad_expert, preferred_element_type=jnp.float32).astype(
        jnp.bfloat16
    )[None]
    grad_gate = jnp.dot(expert_rows.T, grad_gate_pre, preferred_element_type=jnp.float32).astype(
        jnp.bfloat16
    )[None]
    grad_up = jnp.dot(expert_rows.T, grad_up_pre, preferred_element_type=jnp.float32).astype(
        jnp.bfloat16
    )[None]
    input_part = jnp.dot(grad_gate_pre, w_gate[0].T, preferred_element_type=jnp.float32) + jnp.dot(
        grad_up_pre, w_up[0].T, preferred_element_type=jnp.float32
    )
    input_part = input_part.astype(jnp.bfloat16).reshape(ctx_count, capacity, model_width)
    grad_returned = back_from_experts(input_part)
    grad_normed = sum_heads(jnp.sum(pick_rows(grad_returned, route_table), axis=1))
    grad_resid = cot_f32 + rms_back(residual_f32, resid_scale, grad_normed)
    grad_resid_bf = grad_resid.astype(jnp.bfloat16)
    attended_gradient = jnp.dot(
        grad_resid_bf, full_output.T, preferred_element_type=jnp.float32
    ).astype(jnp.bfloat16)
    query_gradients, key_value_gradients = attention_backward(
        query_heads,
        banded_key_span,
        probability_single,
        probability_half,
        attended_gradient.reshape(row_count, kv_heads, query_head_group, HEAD_SIZE),
    )
    rim_grad = shifted(key_value_gradients[:WINDOW].astype(jnp.bfloat16), "ctx", -1).astype(
        jnp.float32
    )
    local_gradient = key_value_gradients[WINDOW:].at[row_count - WINDOW :].add(rim_grad)
    key_value_grad = local_gradient.reshape(row_count, -1).astype(jnp.bfloat16)
    query_grad = query_gradients.reshape(row_count, -1).astype(jnp.bfloat16)
    grad_normed_in = sum_heads(
        jnp.dot(query_grad, full_query.T, preferred_element_type=jnp.float32)
        + jnp.dot(key_value_grad, full_keyval.T, preferred_element_type=jnp.float32)
    )
    grad_tokens = (grad_resid + rms_back(tokens_f32, token_scale, grad_normed_in)).astype(
        jnp.bfloat16
    )
    terms = (
        rounded(jnp.dot(normed.T, query_grad, preferred_element_type=jnp.float32)),
        rounded(jnp.dot(normed.T, key_value_grad, preferred_element_type=jnp.float32)),
        rounded(jnp.dot(attended_flat.T, grad_resid_bf, preferred_element_type=jnp.float32)),
    )
    sum_query, sum_keyval, sum_output = (
        lax.psum_scatter(
            terms[0].astype(jnp.bfloat16), "ctx", scatter_dimension=0, tiled=True
        ).astype(jnp.float32),
        lax.psum_scatter(
            terms[1].astype(jnp.bfloat16), "ctx", scatter_dimension=0, tiled=True
        ).astype(jnp.float32),
        lax.psum_scatter(
            terms[2].astype(jnp.bfloat16), "ctx", scatter_dimension=1, tiled=True
        ).astype(jnp.float32),
    )
    return (
        block_out,
        grad_tokens,
        sum_query.astype(jnp.bfloat16),
        sum_keyval.astype(jnp.bfloat16),
        sum_output.astype(jnp.bfloat16),
        grad_gate,
        grad_up,
        grad_down,
    )


def solution(mesh):
    in_specs = (
        P("ctx", None),
        P("ctx", None),
        P("ctx", None),
        P("ctx", None),
        P("ctx", "exp"),
        P("ctx", "exp"),
        P("exp", "ctx"),
        P("ctx", None, "exp"),
        P("ctx", None, "exp"),
        P("ctx", "exp", None),
    )
    out_specs = (
        P("ctx", None),
        P("ctx", None),
        P("ctx", "exp"),
        P("ctx", "exp"),
        P("exp", "ctx"),
        P("ctx", None, "exp"),
        P("ctx", None, "exp"),
        P("ctx", "exp", None),
    )
    return jax.shard_map(body, mesh=mesh, in_specs=in_specs, out_specs=out_specs, check_vma=False)
```

profile of v0, /device:TPU:82, one launch (start us, length us, event | category | flops | bytes accessed | tf_op | source)
XLA Modules:
  0.0 897.1 jit_solution(17111580672626592761)
XLA Ops:
  16.1 6.2 copy.78
  22.2 6.5 reshape.269
  28.7 8.9 all-to-all-start.2
  38.5 124.4 %all-gather = bf16[32,90,128]{2,1,0:T(8,128)(2,1)} all-gather(bf16[1,90,128]{2,1,0:T(8,128)(2,1)S(1)} %bitcast.179), channel_id=1, replica_groups=mesh['ctx'=32,'exp'=8] {'ctx'}, dimensions={0}, use_global_device_ids=true | all-gather | bytes 760320 | tf_op jit(solution)/shard_map/all_gather | solution.py:127
  172.5 10.1 %all-gather.6.cloned.1.call-done = bf16[32,90,256]{2,1,0:T(8,128)(2,1)} async-done(((bf16[1,90,256]{2,1,0:T(8,128)(2,1)}), bf16[32,90,256]{2,1,0:T(8,128)(2,1)}) %all-gather.6.cloned.1.call-update) | async-done | bytes 1474576 | tf_op jit(solution)/shard_map/all_gather | solution.py:126
  187.8 150.4 %all-gather.8.cloned.1.call-done = bf16[32,90,256]{2,1,0:T(8,128)(2,1)} async-done(((bf16[1,90,256]{2,1,0:T(8,128)(2,1)}), bf16[32,90,256]{2,1,0:T(8,128)(2,1)}) %all-gather.8.cloned.1.call-update) | async-done | bytes 1474576 | tf_op jit(solution)/shard_map/all_gather | solution.py:128
  344.8 81.4 %all-reduce.12.cloned.1.call-done = bf16[128,2880]{0,1:T(8,128)(2,1)} async-done(((bf16[128,2880]{0,1:T(8,128)(2,1)}), bf16[128,2880]{0,1:T(8,128)(2,1)}) %all-reduce.12.cloned.1.call-update) | async-done | bytes 737296 | tf_op jit(solution)/shard_map/psum | solution.py:92
  430.7 6.2 copy.75
  436.9 6.5 reshape.265
  443.4 7.4 all-to-all-start
  450.8 6.5 reshape.270
  457.3 51.7 %all-to-all-done = bf16[32,20,2880]{2,1,0:T(8,128)(2,1)} async-done(((bf16[32,20,2880]{2,1,0:T(8,128)(2,1)}), bf16[32,20,2880]{2,1,0:T(8,128)(2,1)}, u32[]{:S(2)}, u32[]{:S(2)}) %all-to-all-start) | async-done | bytes 3686432 | tf_op jit(solution)/shard_map/all_to_all | solution.py:96
  509.1 6.4 reshape.266
  527.9 6.2 copy.79
  534.1 6.5 reshape.271
  540.6 10.1 %all-to-all-start.3 = ((bf16[32,20,2880]{2,1,0:T(8,128)(2,1)}), bf16[32,20,2880]{2,1,0:T(8,128)(2,1)}, u32[]{:S(2)}, u32[]{:S(2)}) async-start(bf16[32,20,2880]{2,1,0:T(8,128)(2,1)} %reshape.271), calls=%async_computation.3 | async-start | bytes 9043968 | tf_op jit(solution)/shard_map/all_to_all | solution.py:100
  553.8 6.2 copy.76
  560.1 6.4 reshape.267
  566.5 52.8 %all-to-all-done.3 = bf16[32,20,2880]{2,1,0:T(8,128)(2,1)} async-done(((bf16[32,20,2880]{2,1,0:T(8,128)(2,1)}), bf16[32,20,2880]{2,1,0:T(8,128)(2,1)}, u32[]{:S(2)}, u32[]{:S(2)}) %all-to-all-start.3) | async-done | bytes 3686432 | tf_op jit(solution)/shard_map/all_to_all | solution.py:100
  619.3 9.3 %all-to-all-start.1 = ((bf16[32,20,2880]{2,1,0:T(8,128)(2,1)}), bf16[32,20,2880]{2,1,0:T(8,128)(2,1)}, u32[]{:S(2)}, u32[]{:S(2)}) async-start(bf16[32,20,2880]{2,1,0:T(8,128)(2,1)} %reshape.267), calls=%async_computation.1 | async-start | bytes 9043968 | tf_op jit(solution)/shard_map/all_to_all | solution.py:100
  634.7 6.5 reshape.272
  641.2 6.6 fusion.12
  652.5 38.2 %all-to-all-done.1 = bf16[32,20,2880]{2,1,0:T(8,128)(2,1)} async-done(((bf16[32,20,2880]{2,1,0:T(8,128)(2,1)}), bf16[32,20,2880]{2,1,0:T(8,128)(2,1)}, u32[]{:S(2)}, u32[]{:S(2)}) %all-to-all-start.1) | async-done | bytes 3686432 | tf_op jit(solution)/shard_map/all_to_all | solution.py:100
  690.7 6.5 reshape.268
  697.2 6.7 multiply_reduce_fusion
  704.0 18.5 %all-reduce.14.cloned.1.call-done = bf16[128,2880]{0,1:T(8,128)(2,1)} async-done(((bf16[128,2880]{0,1:T(8,128)(2,1)}), bf16[128,2880]{0,1:T(8,128)(2,1)}) %all-reduce.14.cloned.1.call-update) | async-done | bytes 737296 | tf_op jit(solution)/shard_map/psum | solution.py:92
  739.1 95.0 %fusion.78 = (bf16[96,256]{1,0:T(8,128)(2,1)S(1)}, bf16[96,128]{1,0:T(8,128)(2,1)S(1)}, bf16[256,96]{0,1:T(8,128)(2,1)S(1)}) fusion(bf16[2880,256]{1,0:T(8,128)(2,1)S(1)} %convolution_convert_fusion.6, bf16[2880,128]{1,0:T(8,128)(2,1)} %convolution_convert_fusion.7, bf16[256,2880]{0,1:T(8,128)(2,1)} %convolution_convert_fusion.5), kind=kCustom, calls=%all-reduce-scatter.3 | all-reduce-scatter fusion | flops 1966081 | bytes 3810304
  838.4 11.3 %collective-permute-start.5 = (bf16[90,128]{1,0:T(8,128)(2,1)S(1)}, bf16[90,128]{1,0:T(8,128)(2,1)S(1)}, u32[]{:S(2)}, u32[]{:S(2)}) collective-permute-start(bf16[90,128]{1,0:T(8,128)(2,1)S(1)} %slice.57), channel_id=1, source_target_pairs={{0,16},{8,24},{16,32},{24,40},{32,48},{40,56},{48,64},{56,72},{64,... | collective-permute-start | bytes 69128
  849.8 4.8 fusion.8
  858.1 5.4 collective-permute-start.6
  863.5 11.3 %collective-permute-start.7 = (bf16[256,90]{0,1:T(8,128)(2,1)S(1)}, bf16[256,90]{0,1:T(8,128)(2,1)S(1)}, u32[]{:S(2)}, u32[]{:S(2)}) collective-permute-start(bf16[256,90]{0,1:T(8,128)(2,1)S(1)} %slice.58), channel_id=1, source_target_pairs={{0,16},{8,24},{16,32},{24,40},{32,48},{40,56},{48,64},{56,72},{64,... | collective-permute-start | bytes 138248
  877.8 5.4 collective-permute-done.3
  (170 shorter events, 95.3 us)
Async XLA Ops:
  7.2 513.6 %copy-start = (bf16[1,256,2880]{1,2,0:T(8,128)(2,1)S(1)}, bf16[1,256,2880]{1,2,0:T(8,128)(2,1)}, u32[]{:S(2)}) copy-start(bf16[1,256,2880]{1,2,0:T(8,128)(2,1)} %param.23) | copy-start | bytes 4423684
  7.2 175.3 %all-gather.6.cloned.1.call-start = ((), (), s32[]{:S(2)}) async-start(), calls=%async_computation.6 | async-start | bytes 1622016 | tf_op jit(solution)/shard_map/all_gather | solution.py:126
  7.2 4.7 copy-start.31
  7.2 4.7 copy-start.36
  28.7 9.7 %copy-start.30 = (bf16[90,128]{1,0:T(8,128)(2,1)S(1)}, bf16[90,128]{1,0:T(8,128)(2,1)}, u32[]{:S(2)}) copy-start(bf16[90,128]{1,0:T(8,128)(2,1)} %param.19) | copy-start | bytes 69124
  28.7 414.7 %all-to-all-start.2 = ((bf16[32,20,2880]{2,1,0:T(8,128)(2,1)}), bf16[32,20,2880]{2,1,0:T(8,128)(2,1)}, u32[]{:S(2)}, u32[]{:S(2)}) async-start(bf16[32,20,2880]{2,1,0:T(8,128)(2,1)} %reshape.269), calls=%async_computation.2 | async-start | bytes 9043968 | tf_op jit(solution)/shard_map/all_to_all | solution.py:96
  37.6 126.6 %copy-start.2 = (bf16[128,2880]{0,1:T(8,128)(2,1)S(1)}, bf16[128,2880]{0,1:T(8,128)(2,1)}, u32[]{:S(2)}) copy-start(bf16[128,2880]{0,1:T(8,128)(2,1)} %param.14) | copy-start | bytes 2211844
  37.6 300.6 %all-gather.8.cloned.1.call-start = ((), (), s32[]{:S(2)}) async-start(), calls=%async_computation.7 | async-start | bytes 1622016 | tf_op jit(solution)/shard_map/all_gather | solution.py:128
  38.4 387.8 %all-reduce.12.cloned.1.call-start = ((), (), s32[]{:S(2)}) async-start(), calls=%async_computation.4 | async-start | bytes 1474560 | tf_op jit(solution)/shard_map/psum | solution.py:92
  164.2 21.6 %copy-start.12 = (bf16[2880,128]{1,0:T(8,128)(2,1)}, bf16[2880,128]{1,0:T(8,128)(2,1)S(1)}, u32[]{:S(2)}) copy-start(bf16[2880,128]{1,0:T(8,128)(2,1)S(1)} %reshape.276) | copy-start | bytes 2211844
  165.6 6.7 collective-permute-start
  172.4 169.4 %copy-start.27 = (bf16[256,128]{0,1:T(8,128)(2,1)}, bf16[256,128]{0,1:T(8,128)(2,1)S(1)}, u32[]{:S(2)}) copy-start(bf16[256,128]{0,1:T(8,128)(2,1)S(1)} %copy.68) | copy-start | bytes 196612
  187.8 153.8 %copy-start.25 = (bf16[128,256]{0,1:T(8,128)(2,1)}, bf16[128,256]{0,1:T(8,128)(2,1)S(1)}, u32[]{:S(2)}) copy-start(bf16[128,256]{0,1:T(8,128)(2,1)S(1)} %copy.69) | copy-start | bytes 196612
  443.4 65.7 %all-to-all-start = ((bf16[32,20,2880]{2,1,0:T(8,128)(2,1)}), bf16[32,20,2880]{2,1,0:T(8,128)(2,1)}, u32[]{:S(2)}, u32[]{:S(2)}) async-start(bf16[32,20,2880]{2,1,0:T(8,128)(2,1)} %reshape.265), calls=%async_computation | async-start | bytes 9043968 | tf_op jit(solution)/shard_map/all_to_all | solution.py:96
  523.0 27.7 %copy-start.19 = (bf16[640,256]{1,0:T(8,128)(2,1)}, bf16[640,256]{1,0:T(8,128)(2,1)S(1)}, u32[]{:S(2)}) copy-start(bf16[640,256]{1,0:T(8,128)(2,1)S(1)} %get-tuple-element.40) | copy-start | bytes 983044
  540.6 78.8 %all-to-all-start.3 = ((bf16[32,20,2880]{2,1,0:T(8,128)(2,1)}), bf16[32,20,2880]{2,1,0:T(8,128)(2,1)}, u32[]{:S(2)}, u32[]{:S(2)}) async-start(bf16[32,20,2880]{2,1,0:T(8,128)(2,1)} %reshape.271), calls=%async_computation.3 | async-start | bytes 9043968 | tf_op jit(solution)/shard_map/all_to_all | solution.py:100
  566.5 62.4 %copy-start.35 = (u32[256]{0:T(256)S(1)}, u32[256]{0:T(256)}, u32[]{:S(2)}) copy-start(u32[256]{0:T(256)} %constant.82) | copy-start | bytes 3076
  566.5 63.6 %copy-start.22 = (bf16[640,256]{1,0:T(8,128)(2,1)S(1)}, bf16[640,256]{1,0:T(8,128)(2,1)}, u32[]{:S(2)}) copy-start(bf16[640,256]{1,0:T(8,128)(2,1)} %copy-done.21) | copy-start | bytes 983044
  619.3 71.4 %all-to-all-start.1 = ((bf16[32,20,2880]{2,1,0:T(8,128)(2,1)}), bf16[32,20,2880]{2,1,0:T(8,128)(2,1)}, u32[]{:S(2)}, u32[]{:S(2)}) async-start(bf16[32,20,2880]{2,1,0:T(8,128)(2,1)} %reshape.267), calls=%async_computation.1 | async-start | bytes 9043968 | tf_op jit(solution)/shard_map/all_to_all | solution.py:100
  628.6 93.9 %all-reduce.14.cloned.1.call-start = ((), (), s32[]{:S(2)}) async-start(), calls=%async_computation.5 | async-start | bytes 1474560 | tf_op jit(solution)/shard_map/psum | solution.py:92
  641.2 6.7 copy-start.24
  647.9 237.5 %all-reduce.16.cloned.1.call-start = ((), (), s32[]{:S(2)}) async-start(), calls=%async_computation.8 | async-start | bytes 2949120 | tf_op jit(solution)/shard_map/psum | solution.py:92
  704.0 20.6 %copy-start.4 = (bf16[128,2880]{0,1:T(8,128)(2,1)S(1)}, bf16[128,2880]{0,1:T(8,128)(2,1)}, u32[]{:S(2)}) copy-start(bf16[128,2880]{0,1:T(8,128)(2,1)} %param.15) | copy-start | bytes 2211844
  730.8 5.8 collective-permute-start.1
  739.1 110.7 %copy-start.20 = (bf16[640,256]{1,0:T(8,128)(2,1)S(1)}, bf16[640,256]{1,0:T(8,128)(2,1)}, u32[]{:S(2)}) copy-start(bf16[640,256]{1,0:T(8,128)(2,1)} %copy-done.19) | copy-start | bytes 983044
  834.1 42.6 %collective-permute-start.4 = (bf16[96,128]{1,0:T(8,128)(2,1)S(1)}, bf16[96,128]{1,0:T(8,128)(2,1)S(1)}, u32[]{:S(2)}, u32[]{:S(2)}) collective-permute-start(bf16[96,128]{1,0:T(8,128)(2,1)S(1)} %get-tuple-element.34), channel_id=1, source_target_pairs={{0,8},{8,16},{16,24},{24,32},{32,40},{40,48},{48,56},{56,64},{64,7... | collective-permute-start | bytes 73736
  838.4 36.4 %collective-permute-start.5 = (bf16[90,128]{1,0:T(8,128)(2,1)S(1)}, bf16[90,128]{1,0:T(8,128)(2,1)S(1)}, u32[]{:S(2)}, u32[]{:S(2)}) collective-permute-start(bf16[90,128]{1,0:T(8,128)(2,1)S(1)} %slice.57), channel_id=1, source_target_pairs={{0,16},{8,24},{16,32},{24,40},{32,48},{40,56},{48,64},{56,72},{64,... | collective-permute-start | bytes 69128
  854.6 32.5 %copy-start.34 = (f32[128]{0:T(128)S(1)}, f32[128]{0:T(128)}, u32[]{:S(2)}) copy-start(f32[128]{0:T(128)} %get-tuple-element.43) | copy-start | bytes 1540
  854.6 28.6 %collective-permute-start.2 = (bf16[96,256]{1,0:T(8,128)(2,1)S(1)}, bf16[96,256]{1,0:T(8,128)(2,1)S(1)}, u32[]{:S(2)}, u32[]{:S(2)}) collective-permute-start(bf16[96,256]{1,0:T(8,128)(2,1)S(1)} %get-tuple-element.33), channel_id=1, source_target_pairs={{0,8},{8,16},{16,24},{24,32},{32,40},{40,48},{48,56},{56,64},{64,7... | collective-permute-start | bytes 147464
  858.1 25.6 %collective-permute-start.6 = (bf16[256,96]{0,1:T(8,128)(2,1)S(1)}, bf16[256,96]{0,1:T(8,128)(2,1)S(1)}, u32[]{:S(2)}, u32[]{:S(2)}) collective-permute-start(bf16[256,96]{0,1:T(8,128)(2,1)S(1)} %get-tuple-element.35), channel_id=1, source_target_pairs={{0,8},{8,16},{16,24},{24,32},{32,40},{40,48},{48,56},{56,64},{64,7... | collective-permute-start | bytes 147464
  863.5 20.2 %collective-permute-start.7 = (bf16[256,90]{0,1:T(8,128)(2,1)S(1)}, bf16[256,90]{0,1:T(8,128)(2,1)S(1)}, u32[]{:S(2)}, u32[]{:S(2)}) collective-permute-start(bf16[256,90]{0,1:T(8,128)(2,1)S(1)} %slice.58), channel_id=1, source_target_pairs={{0,16},{8,24},{16,32},{24,40},{32,48},{40,56},{48,64},{56,72},{64,... | collective-permute-start | bytes 138248
  874.8 8.4 collective-permute-start.3
  (22 other events, 48.3 us)
Sparse Core Ops, SparseCore 0:
  9.8 172.6 all-gather.5
  184.3 153.8 all-gather.7
  344.7 81.4 all-reduce.11
  648.0 74.3 all-reduce.13
  739.2 84.5 all-reduce.15
where the time goes:
time: 900 us; the launch traced here: 897 us
  waiting for transfers between devices  413 us (46%)
  blocking collectives  219 us (24%)
  local copies, waits for them, and re-layouts  95.2 us (11%)
  starting transfers between devices  80.3 us (9%)
  matrix products  61.4 us (7%)
  between operations  15.1 us (2%)
  other arithmetic  12.2 us (1%)
    all_gather x1, waiting for transfers between devices, body(): lax.all_gather(w_output, 'ctx', axis=1, tiled=True)  150 us
    all_gather x1, blocking collectives, body(): lax.all_gather(key_value_weight, 'ctx', axis=0, tiled=True)  124 us
    psum x3, waiting for transfers between devices, sum_heads(): return lax.psum(values.astype(jnp.bfloat16), 'exp').astype(jnp.float32)  99.9 us
    unnamed x1, blocking collectives  95 us
    all_to_all x2, waiting for transfers between devices, back_from_experts(): lax.all_to_all(buffer, 'ctx', split_axis=0, concat_axis=0, tiled=True)  91 us
    all_to_all x2, waiting for transfers between devices, over_experts(): lax.all_to_all(buffer, 'ctx', split_axis=0, concat_axis=0, tiled=True)  51.7 us
    unnamed x6, starting transfers between devices  37.7 us
    all_to_all x2, starting transfers between devices, back_from_experts(): lax.all_to_all(buffer, 'ctx', split_axis=0, concat_axis=0, tiled=True)  19.3 us
  transfers between devices with their start and end apart: 17, of which 10 were waited for; matrix products, arithmetic and copies ran while one was open for 24% of the time, Pallas kernels for 0%

commit v1 on v0

--- a/solution.py
+++ b/solution.py
@@ -89,7 +89,7 @@
 
 
 def sum_heads(values):
-    return lax.psum(values.astype(jnp.bfloat16), "exp").astype(jnp.float32)
+    return jnp.sum(lax.all_gather(values.astype(jnp.bfloat16), "exp"), axis=0).astype(jnp.float32)
 
 
 def over_experts(buffer):

time: 900 us -> 1050 us (1.17)
  blocking collectives: 219 us -> 349 us
  other arithmetic: 12.2 us -> 57.8 us
  waiting for transfers between devices: 413 us -> 381 us
  local copies, waits for them, and re-layouts: 95.2 us -> 113 us
  starting transfers between devices: 80.3 us -> 66.9 us
    all_to_all x0 -> x2, blocking collectives: none -> 156 us  [back_from_experts(): lax.all_to_all(buffer, 'ctx', split_axis=0, concat_axis=0, tiled=True)]
    psum x3 -> x0, waiting for transfers between devices: 99.9 us -> none  [sum_heads(): return lax.psum(values.astype(jnp.bfloat16), 'exp').astype(jnp.float32)]
    all_gather x0 -> x4, waiting for transfers between devices: none -> 98.8 us  [sum_heads(): lax.all_gather(values.astype(jnp.bfloat16), 'exp')]
    all_to_all x2 -> x0, waiting for transfers between devices: 91 us -> none  [back_from_experts(): lax.all_to_all(buffer, 'ctx', split_axis=0, concat_axis=0, tiled=True)]
    all_gather x1, waiting for transfers between devices: 10.1 us -> 66.5 us  [body(): lax.all_gather(w_query, 'ctx', axis=0, tiled=True)]
    reduce_sum x0 -> x4, other arithmetic: none -> 51.6 us  [sum_heads(): jnp.sum(lax.all_gather(values.astype(jnp.bfloat16), 'exp'), axis=0)]
    all_gather x1, blocking collectives: 124 us -> 74.2 us  [body(): lax.all_gather(key_value_weight, 'ctx', axis=0, tiled=True)]
    unnamed x1, blocking collectives: 95 us -> 119 us
  transfers between devices with their start and end apart: 17 -> 16, of which waited for: 10 -> 8; matrix products, arithmetic and copies ran while one was open for 24% -> 27% of each run, Pallas kernels for 0% -> 0%
where the time goes in v1:
time: 1050 us; the launch traced here: 1040 us
  waiting for transfers between devices  381 us (36%)
  blocking collectives  349 us (33%)
  local copies, waits for them, and re-layouts  113 us (11%)
  starting transfers between devices  66.9 us (6%)
  matrix products  59.1 us (6%)
  other arithmetic  57.8 us (6%)
  between operations  16 us (2%)
    all_to_all x2, blocking collectives, back_from_experts(): lax.all_to_all(buffer, 'ctx', split_axis=0, concat_axis=0, tiled=True)  156 us
    all_gather x1, waiting for transfers between devices, body(): lax.all_gather(w_output, 'ctx', axis=1, tiled=True)  151 us
    unnamed x1, blocking collectives  119 us
    all_gather x4, waiting for transfers between devices, sum_heads(): lax.all_gather(values.astype(jnp.bfloat16), 'exp')  98.8 us
    all_gather x1, blocking collectives, body(): lax.all_gather(key_value_weight, 'ctx', axis=0, tiled=True)  74.2 us
    all_gather x1, waiting for transfers between devices, body(): lax.all_gather(w_query, 'ctx', axis=0, tiled=True)  66.5 us
    all_to_all x2, waiting for transfers between devices, over_experts(): lax.all_to_all(buffer, 'ctx', split_axis=0, concat_axis=0, tiled=True)  55.1 us
    reduce_sum x4, other arithmetic, sum_heads(): jnp.sum(lax.all_gather(values.astype(jnp.bfloat16), 'exp'), axis=0)  51.6 us
  transfers between devices with their start and end apart: 16, of which 8 were waited for; matrix products, arithmetic and copies ran while one was open for 27% of the time, Pallas kernels for 0%

profile of v1, /device:TPU:82, one launch (start us, length us, event | category | flops | bytes accessed | tf_op | source)
XLA Modules:
  0.0 1043.2 jit_solution(212107295934894280)
XLA Ops:
  8.7 74.2 %all-gather.4 = bf16[32,90,128]{2,1,0:T(8,128)(2,1)} all-gather(bf16[1,90,128]{2,1,0:T(8,128)(2,1)} %bitcast.203), channel_id=1, replica_groups=mesh['ctx'=32,'exp'=8] {'ctx'}, dimensions={0}, use_global_device_ids=true | all-gather | bytes 760320 | tf_op jit(solution)/shard_map/all_gather | solution.py:127
  91.9 66.5 %all-gather.22.cloned.1.call-done = bf16[32,90,256]{2,1,0:T(8,128)(2,1)} async-done(((bf16[1,90,256]{2,1,0:T(8,128)(2,1)}), bf16[32,90,256]{2,1,0:T(8,128)(2,1)}) %all-gather.22.cloned.1.call-update) | async-done | bytes 1474576 | tf_op jit(solution)/shard_map/all_gather | solution.py:126
  164.1 151.2 %all-gather.24.cloned.1.call-done = bf16[32,90,256]{2,1,0:T(8,128)(2,1)} async-done(((bf16[1,90,256]{2,1,0:T(8,128)(2,1)}), bf16[32,90,256]{2,1,0:T(8,128)(2,1)}) %all-gather.24.cloned.1.call-update) | async-done | bytes 1474576 | tf_op jit(solution)/shard_map/all_gather | solution.py:128
  328.0 6.2 copy.78
  334.2 6.4 reshape.285
  340.6 16.4 %all-to-all-start.2 = ((bf16[32,20,2880]{2,1,0:T(8,128)(2,1)}), bf16[32,20,2880]{2,1,0:T(8,128)(2,1)}, u32[]{:S(2)}, u32[]{:S(2)}) async-start(bf16[32,20,2880]{2,1,0:T(8,128)(2,1)} %reshape.285), calls=%async_computation.2 | async-start | bytes 9043968 | tf_op jit(solution)/shard_map/all_to_all | solution.py:96
  357.3 68.4 %all-gather.14.cloned.1.call-done = bf16[1024,2880]{0,1:T(8,128)(2,1)} async-done(((bf16[128,2880]{0,1:T(8,128)(2,1)}), bf16[1024,2880]{0,1:T(8,128)(2,1)}) %all-gather.14.cloned.1.call-update) | async-done | bytes 5898256 | tf_op jit(solution)/shard_map/all_gather | solution.py:92
  429.9 12.3 %bitcast_reduce_fusion.3 = bf16[128,2880]{0,1:T(8,128)(2,1)S(1)} fusion(bf16[360,8,8,128]{3,2,1,0:T(8,128)(2,1)S(1)} %copy.94), kind=kLoop, calls=%fused_computation.5 | loop fusion | flops 2580480 | bytes 6635520 | tf_op jit(solution)/shard_map/reduce_sum | solution.py:92
  445.5 6.2 copy.75
  451.6 6.4 reshape.281
  458.1 7.4 all-to-all-start
  466.0 6.5 reshape.286
  472.5 55.1 %all-to-all-done = bf16[32,20,2880]{2,1,0:T(8,128)(2,1)} async-done(((bf16[32,20,2880]{2,1,0:T(8,128)(2,1)}), bf16[32,20,2880]{2,1,0:T(8,128)(2,1)}, u32[]{:S(2)}, u32[]{:S(2)}) %all-to-all-start) | async-done | bytes 3686432 | tf_op jit(solution)/shard_map/all_to_all | solution.py:96
  527.6 6.5 reshape.282
  546.4 6.2 copy.79
  552.7 6.4 reshape.287
  559.1 59.9 %all_to_all.20 = bf16[32,20,2880]{2,1,0:T(8,128)(2,1)} all-to-all(bf16[32,20,2880]{2,1,0:T(8,128)(2,1)} %reshape.287), channel_id=1, replica_groups=mesh['ctx'=32,'exp'=8] {'ctx'}, dimensions={0} | all-to-all | bytes 7372800 | tf_op jit(solution)/shard_map/all_to_all | solution.py:100
  619.0 6.5 reshape.288
  625.4 6.6 fusion.12
  635.3 6.2 copy.76
  641.5 6.5 reshape.283
  647.9 96.4 %all_to_all.21 = bf16[32,20,2880]{2,1,0:T(8,128)(2,1)} all-to-all(bf16[32,20,2880]{2,1,0:T(8,128)(2,1)} %reshape.283), channel_id=1, replica_groups=mesh['ctx'=32,'exp'=8] {'ctx'}, dimensions={0} | all-to-all | bytes 7372800 | tf_op jit(solution)/shard_map/all_to_all | solution.py:100
  744.4 6.5 reshape.284
  750.9 6.7 multiply_reduce_fusion
  761.9 12.3 %bitcast_reduce_fusion.1 = bf16[128,2880]{0,1:T(8,128)(2,1)S(1)} fusion(bf16[360,8,8,128]{3,2,1,0:T(8,128)(2,1)S(1)} %copy.96), kind=kLoop, calls=%fused_computation.3 | loop fusion | flops 2580480 | bytes 6635520 | tf_op jit(solution)/shard_map/reduce_sum | solution.py:92
  798.9 30.4 %all-gather.16.cloned.1.call-done = bf16[1024,2880]{0,1:T(8,128)(2,1)} async-done(((bf16[128,2880]{0,1:T(8,128)(2,1)}), bf16[1024,2880]{0,1:T(8,128)(2,1)}) %all-gather.16.cloned.1.call-update) | async-done | bytes 5898256 | tf_op jit(solution)/shard_map/all_gather | solution.py:92
  829.3 6.8 copy.95
  839.6 118.6 %fusion.78 = (bf16[96,256]{1,0:T(8,128)(2,1)S(1)}, bf16[96,128]{1,0:T(8,128)(2,1)S(1)}, bf16[256,96]{0,1:T(8,128)(2,1)S(1)}) fusion(bf16[2880,256]{1,0:T(8,128)(2,1)S(1)} %convolution_convert_fusion.6, bf16[2880,128]{1,0:T(8,128)(2,1)} %convolution_convert_fusion.7, bf16[256,2880]{0,1:T(8,128)(2,1)} %convolution_convert_fusion.5), kind=kCustom, calls=%all-reduce-scatter.3 | all-reduce-scatter fusion | flops 1966081 | bytes 3810304
  961.0 10.2 collective-permute-start.5
  971.2 14.7 %bitcast_reduce_fusion.2 = bf16[128,2880]{0,1:T(8,128)(2,1)} fusion(bf16[360,8,8,128]{3,2,1,0:T(8,128)(2,1)} %copy.95), kind=kLoop, calls=%fused_computation.4 | loop fusion | flops 2580480 | bytes 6635520 | tf_op jit(solution)/shard_map/reduce_sum | solution.py:92
  993.7 11.8 %collective-permute-start.7 = (bf16[256,90]{0,1:T(8,128)(2,1)S(1)}, bf16[256,90]{0,1:T(8,128)(2,1)S(1)}, u32[]{:S(2)}, u32[]{:S(2)}) collective-permute-start(bf16[256,90]{0,1:T(8,128)(2,1)S(1)} %slice.58), channel_id=1, source_target_pairs={{0,16},{8,24},{16,32},{24,40},{32,48},{40,56},{48,64},{56,72},{64,... | collective-permute-start | bytes 138248
  1020.3 12.3 %bitcast_reduce_fusion = bf16[128,2880]{0,1:T(8,128)(2,1)S(1)} fusion(bf16[360,8,8,128]{3,2,1,0:T(8,128)(2,1)S(1)} %copy.97), kind=kLoop, calls=%fused_computation.2 | loop fusion | flops 2580480 | bytes 6635520 | tf_op jit(solution)/shard_map/reduce_sum | solution.py:92
  (183 shorter events, 112.5 us)
Async XLA Ops:
  7.2 532.2 %copy-start = (bf16[1,256,2880]{1,2,0:T(8,128)(2,1)S(1)}, bf16[1,256,2880]{1,2,0:T(8,128)(2,1)}, u32[]{:S(2)}) copy-start(bf16[1,256,2880]{1,2,0:T(8,128)(2,1)} %param.23) | copy-start | bytes 4423684
  7.2 77.1 %copy-start.2 = (bf16[128,2880]{0,1:T(8,128)(2,1)S(1)}, bf16[128,2880]{0,1:T(8,128)(2,1)}, u32[]{:S(2)}) copy-start(bf16[128,2880]{0,1:T(8,128)(2,1)} %param.14) | copy-start | bytes 2211844
  7.2 151.1 %all-gather.22.cloned.1.call-start = ((), (), s32[]{:S(2)}) async-start(), calls=%async_computation.8 | async-start | bytes 1622016 | tf_op jit(solution)/shard_map/all_gather | solution.py:126
  7.9 307.4 %all-gather.24.cloned.1.call-start = ((), (), s32[]{:S(2)}) async-start(), calls=%async_computation.9 | async-start | bytes 1622016 | tf_op jit(solution)/shard_map/all_gather | solution.py:128
  8.7 417.0 %all-gather.14.cloned.1.call-start = ((), (), s32[]{:S(2)}) async-start(), calls=%async_computation.4 | async-start | bytes 6635520 | tf_op jit(solution)/shard_map/all_gather | solution.py:92
  84.2 77.4 %copy-start.16 = (bf16[2880,128]{1,0:T(8,128)(2,1)}, bf16[2880,128]{1,0:T(8,128)(2,1)S(1)}, u32[]{:S(2)}) copy-start(bf16[2880,128]{1,0:T(8,128)(2,1)S(1)} %reshape.296) | copy-start | bytes 2211844
  85.7 6.1 collective-permute-start
  91.8 72.1 %copy-start.30 = (bf16[256,128]{0,1:T(8,128)(2,1)}, bf16[256,128]{0,1:T(8,128)(2,1)S(1)}, u32[]{:S(2)}) copy-start(bf16[256,128]{0,1:T(8,128)(2,1)S(1)} %copy.68) | copy-start | bytes 196612
  163.6 155.1 %copy-start.28 = (bf16[128,256]{0,1:T(8,128)(2,1)}, bf16[128,256]{0,1:T(8,128)(2,1)S(1)}, u32[]{:S(2)}) copy-start(bf16[128,256]{0,1:T(8,128)(2,1)S(1)} %copy.69) | copy-start | bytes 196612
  163.9 154.8 %copy-start.20 = (f32[1,4,128,256]{2,3,1,0:T(8,128)}, f32[1,4,128,256]{2,3,1,0:T(8,128)S(1)}, u32[]{:S(2)}) copy-start(f32[1,4,128,256]{2,3,1,0:T(8,128)S(1)} %get-tuple-element.46) | copy-start | bytes 1572868
  340.6 117.4 %all-to-all-start.2 = ((bf16[32,20,2880]{2,1,0:T(8,128)(2,1)}), bf16[32,20,2880]{2,1,0:T(8,128)(2,1)}, u32[]{:S(2)}, u32[]{:S(2)}) async-start(bf16[32,20,2880]{2,1,0:T(8,128)(2,1)} %reshape.285), calls=%async_computation.2 | async-start | bytes 9043968 | tf_op jit(solution)/shard_map/all_to_all | solution.py:96
  458.1 69.5 %all-to-all-start = ((bf16[32,20,2880]{2,1,0:T(8,128)(2,1)}), bf16[32,20,2880]{2,1,0:T(8,128)(2,1)}, u32[]{:S(2)}, u32[]{:S(2)}) async-start(bf16[32,20,2880]{2,1,0:T(8,128)(2,1)} %reshape.281), calls=%async_computation | async-start | bytes 9043968 | tf_op jit(solution)/shard_map/all_to_all | solution.py:96
  465.5 292.2 %all-gather.18.cloned.1.call-start = ((), (), s32[]{:S(2)}) async-start(), calls=%async_computation.6 | async-start | bytes 6635520 | tf_op jit(solution)/shard_map/all_gather | solution.py:92
  541.6 90.6 %copy-start.22 = (bf16[640,256]{1,0:T(8,128)(2,1)}, bf16[640,256]{1,0:T(8,128)(2,1)S(1)}, u32[]{:S(2)}) copy-start(bf16[640,256]{1,0:T(8,128)(2,1)S(1)} %get-tuple-element.38) | copy-start | bytes 983044
  632.1 197.2 %all-gather.16.cloned.1.call-start = ((), (), s32[]{:S(2)}) async-start(), calls=%async_computation.5 | async-start | bytes 6635520 | tf_op jit(solution)/shard_map/all_gather | solution.py:92
  757.6 258.5 %all-gather.20.cloned.1.call-start = ((), (), s32[]{:S(2)}) async-start(), calls=%async_computation.7 | async-start | bytes 6635520 | tf_op jit(solution)/shard_map/all_gather | solution.py:92
  761.9 13.3 %copy-start.11 = (bf16[2880,256]{1,0:T(8,128)(2,1)S(1)}, bf16[2880,256]{1,0:T(8,128)(2,1)}, u32[]{:S(2)}) copy-start(bf16[2880,256]{1,0:T(8,128)(2,1)} %reshape.300) | copy-start | bytes 4423684
  779.1 5.1 copy-start.31
  779.1 5.2 copy-start.3
  780.5 5.8 collective-permute-start.1
  788.9 5.0 copy-start.14
  788.9 5.0 copy-start.25
  829.3 6.8 copy-start.5
  829.3 6.8 copy-start.9
  829.3 6.8 copy-start.35
  958.3 49.1 %collective-permute-start.4 = (bf16[96,128]{1,0:T(8,128)(2,1)S(1)}, bf16[96,128]{1,0:T(8,128)(2,1)S(1)}, u32[]{:S(2)}, u32[]{:S(2)}) collective-permute-start(bf16[96,128]{1,0:T(8,128)(2,1)S(1)} %get-tuple-element.32), channel_id=1, source_target_pairs={{0,8},{8,16},{16,24},{24,32},{32,40},{40,48},{48,56},{56,64},{64,7... | collective-permute-start | bytes 73736
  961.0 44.5 %collective-permute-start.5 = (bf16[90,128]{1,0:T(8,128)(2,1)S(1)}, bf16[90,128]{1,0:T(8,128)(2,1)S(1)}, u32[]{:S(2)}, u32[]{:S(2)}) collective-permute-start(bf16[90,128]{1,0:T(8,128)(2,1)S(1)} %slice.57), channel_id=1, source_target_pairs={{0,16},{8,24},{16,32},{24,40},{32,48},{40,56},{48,64},{56,72},{64,... | collective-permute-start | bytes 69128
  985.9 27.9 %collective-permute-start.2 = (bf16[96,256]{1,0:T(8,128)(2,1)S(1)}, bf16[96,256]{1,0:T(8,128)(2,1)S(1)}, u32[]{:S(2)}, u32[]{:S(2)}) collective-permute-start(bf16[96,256]{1,0:T(8,128)(2,1)S(1)} %get-tuple-element.31), channel_id=1, source_target_pairs={{0,8},{8,16},{16,24},{24,32},{32,40},{40,48},{48,56},{56,64},{64,7... | collective-permute-start | bytes 147464
  988.7 25.6 %collective-permute-start.6 = (bf16[256,96]{0,1:T(8,128)(2,1)S(1)}, bf16[256,96]{0,1:T(8,128)(2,1)S(1)}, u32[]{:S(2)}, u32[]{:S(2)}) collective-permute-start(bf16[256,96]{0,1:T(8,128)(2,1)S(1)} %get-tuple-element.33), channel_id=1, source_target_pairs={{0,8},{8,16},{16,24},{24,32},{32,40},{40,48},{48,56},{56,64},{64,7... | collective-permute-start | bytes 147464
  993.7 20.7 %collective-permute-start.7 = (bf16[256,90]{0,1:T(8,128)(2,1)S(1)}, bf16[256,90]{0,1:T(8,128)(2,1)S(1)}, u32[]{:S(2)}, u32[]{:S(2)}) collective-permute-start(bf16[256,90]{0,1:T(8,128)(2,1)S(1)} %slice.58), channel_id=1, source_target_pairs={{0,16},{8,24},{16,32},{24,40},{32,48},{40,56},{48,64},{56,72},{64,... | collective-permute-start | bytes 138248
  1005.5 8.4 collective-permute-start.3
  1020.3 12.8 %copy-start.15 = (bf16[128,2880]{0,1:T(8,128)(2,1)S(1)}, bf16[128,2880]{0,1:T(8,128)(2,1)}, u32[]{:S(2)}) copy-start(bf16[128,2880]{0,1:T(8,128)(2,1)} %bitcast_reduce_fusion.2) | copy-start | bytes 2211844
  (23 other events, 47.9 us)
Sparse Core Ops, SparseCore 0:
  9.8 148.4 all-gather.21
  160.1 155.1 all-gather.23
  321.7 103.9 all-gather.13
  632.2 88.3 all-gather.17
  757.7 71.5 all-gather.15
  831.6 69.9 all-gather.19
